TPU v7x, 32 devices: a whole 2x2x4 slice. The times are simulated.
32 devices in a mesh: groups: 2 (over y), feat: 4 (over z), dp: 4 (over x, core).
Axes of the slice: x: 2, y: 2, z: 4, core: 2. Of those that a mesh axis runs over, the one named last changes fastest.
Arguments:
- features: bfloat16 [2048, 8192], P(('groups', 'dp'), 'feat'), parts along dimension 0, may hold values from -6 to 6
- bn_gain: float32 [8192], P('feat'), may hold values from 0.1 to 1.9
- bn_shift: float32 [8192], P('feat'), may hold values from -0.5 to 0.5
- weight: bfloat16 [8192, 8192], P('feat'), may hold values from -2 to 2
Outputs:
- covariance: float32 [16384, 8192], P(('groups', 'dp'), 'feat'), parts along dimension 0
- grad_in: bfloat16 [2048, 8192], P(('groups', 'dp'), 'feat'), parts along dimension 0
There are 2 independent parts, one for each index of `groups`. A program takes and returns all parts, laid end to end along the dimension named above; an argument that names none is the same for every part. Nothing has to cross between parts.
All inputs are finite; a program needn't handle non-finite values.
Results may differ from a plain program's by a relative error of at most 0.014.
Values may be sent and summed in bfloat16 or wider, within the bound.
A program may use at most 256 MiB of HBM per device.

v0:
```python
import jax
import jax.numpy as jnp
from jax import lax
from jax.sharding import PartitionSpec as P


def whole_rows(centered):
    return lax.all_gather(centered, "feat", axis=1, tiled=True)


def shards(features, bn_gain, bn_shift, weight):
    dp_count = lax.axis_size("dp")
    feat_count = lax.axis_size("feat")
    local_rows = features.shape[0]
    images = local_rows * dp_count
    hidden = features.astype(jnp.float32)
    col_sums, col_squares = lax.psum((jnp.sum(hidden, 0), jnp.sum(hidden * hidden, 0)), "dp")
    mean_h = col_sums / images
    var_h = col_squares / images - mean_h * mean_h
    normed = (hidden - mean_h) * lax.rsqrt(var_h + 1e-05) * bn_gain + bn_shift
    activated = jnp.maximum(normed, 0.0).astype(jnp.bfloat16)
    partial_value = jnp.dot(activated, weight, preferred_element_type=jnp.float32)
    projected = lax.psum_scatter(partial_value, "feat", scatter_dimension=1, tiled=True).astype(
        jnp.bfloat16
    )
    proj_f = projected.astype(jnp.float32)
    proj_mean = lax.psum(jnp.sum(proj_f, 0), "dp") / images
    centered = (proj_f - proj_mean).astype(jnp.bfloat16)
    cent_f = centered.astype(jnp.float32)
    width_f = centered.shape[1]
    width_x = width_f * feat_count // dp_count
    cent_full = None
    cent_full = whole_rows(centered)
    cent_x = lax.all_to_all(cent_full, "dp", split_axis=1, concat_axis=0, tiled=True)
    piece = lax.all_gather(centered, "dp", axis=0, tiled=True)
    cov_tile = lax.dot_general(
        cent_x, piece, (((0,), (0,)), ((), ())), preferred_element_type=jnp.float32
    )
    piece_f = piece.astype(jnp.float32)
    cov_tile, sq_sum = (cov_tile, jnp.sum(piece_f * piece_f, 0))
    covariance = cov_tile / (images - 1)
    proj_var = sq_sum / (images - 1)
    spread = jnp.sqrt(proj_var + 0.0001)
    row_ids = lax.axis_index("dp") * width_x + jnp.arange(width_x, dtype=jnp.int32)[:, None]
    col_ids = lax.axis_index("feat") * width_f + jnp.arange(width_f, dtype=jnp.int32)[None, :]
    off_diag = jnp.where(row_ids == col_ids, 0.0, covariance).astype(jnp.bfloat16)
    mixed = jnp.dot(
        cent_full,
        lax.all_gather(off_diag, "dp", axis=0, tiled=True),
        preferred_element_type=jnp.float32,
    )
    scale_up = images / (images - 1)
    active = jnp.where(spread < 1.0, 1.0 / spread, 0.0)
    grad_proj = (4.0 * scale_up * mixed - 25.0 * scale_up * active * cent_f).astype(jnp.bfloat16)
    grad_in = lax.dot_general(
        lax.all_gather(grad_proj, "feat", axis=1, tiled=True),
        weight,
        (((1,), (1,)), ((), ())),
        preferred_element_type=jnp.float32,
    )
    return (covariance, grad_in.astype(jnp.bfloat16))


def solution(mesh):
    in_specs = (P(("groups", "dp"), "feat"), P("feat"), P("feat"), P("feat", None))
    out_specs = (P(("groups", "dp"), "feat"), P(("groups", "dp"), "feat"))
    return jax.shard_map(shards, mesh=mesh, in_specs=in_specs, out_specs=out_specs, check_vma=False)
```

profile of v0, /device:TPU:0, one launch (start us, length us, event | category | flops | bytes accessed | tf_op | source)
XLA Modules:
  0.0 694.4 jit_solution(14080801374418411626)
XLA Ops:
  7.2 0.0 reduce-scatter.2.cloned.1.call-start
  7.2 1.5 convert_reduce_fusion
  8.7 12.7 %all-reduce = (f32[2048]{0:T(1024)S(1)}, f32[2048]{0:T(1024)S(1)}) all-reduce(f32[2048]{0:T(1024)S(1)} %get-tuple-element.3, f32[2048]{0:T(1024)S(1)} %get-tuple-element.2), channel_id=1, replica_groups=mesh['groups'=2,'feat'=4,'dp'=4] {'dp'}, use_global_device_ids=true, to_apply=%region_3.0 | all-reduce | flops 4096 | bytes 32768 | tf_op jit(solution)/shard_map/psum | solution.py:17
  21.4 17.4 %fusion.9 = f32[256,8192]{1,0:T(8,128)} fusion(bf16[2048,8192]{1,0:T(8,128)(2,1)} %param.7, bf16[256,2048]{1,0:T(8,128)(2,1)} %param.4, f32[2048]{0:T(1024)} %param.6, f32[2048]{0:T(1024)} %param.5, f32[2048]{0:T(1024)S(1)} %get-tuple-element.7, f32[2048]{0:T(1024)S(1)} %get-tuple-element.6), kind=kOutput, calls=%fused_computation.20 | convolution fusion | flops 8593604608 | bytes 43024384 | tf_op jit(solution)/shard_map/dot_general | solution.py:22
  38.8 0.0 reduce-scatter.2.cloned.1.call-update
  38.9 0.0 all-gather.5.cloned.1.call-start
  38.9 144.9 %reduce-scatter.2.cloned.1.call-done = f32[256,2048]{1,0:T(8,128)} async-done(((f32[256,8192]{1,0:T(8,128)}), f32[256,2048]{1,0:T(8,128)}) %reduce-scatter.2.cloned.1.call-update) | async-done | bytes 2097168 | tf_op jit(solution)/shard_map/reduce_scatter | solution.py:23
  183.8 1.7 convert_reduce_fusion.1
  185.5 6.5 psum.23
  192.0 2.7 fusion.2
  194.8 0.0 all-gather.5.cloned.1.call-update
  194.8 0.0 all-gather.7.cloned.1.call-start
  194.9 0.7 all-gather.7.cloned.1.call-update
  195.6 80.5 %all-gather.5.cloned.1.call-done = bf16[256,8192]{1,0:T(8,128)(2,1)} async-done(((bf16[256,2048]{1,0:T(8,128)(2,1)}), bf16[256,8192]{1,0:T(8,128)(2,1)}) %all-gather.5.cloned.1.call-update) | async-done | bytes 4194320 | tf_op jit(solution)/shard_map/all_gather | solution.py:8
  276.0 4.8 copy.9
  280.8 4.9 all-to-all-start
  285.8 0.0 all-gather.9.cloned.1.call-start
  285.8 46.1 %all-gather.7.cloned.1.call-done = bf16[1024,2048]{1,0:T(8,128)(2,1)} async-done(((bf16[256,2048]{1,0:T(8,128)(2,1)}), bf16[1024,2048]{1,0:T(8,128)(2,1)}) %all-gather.7.cloned.1.call-update) | async-done | bytes 4194320 | tf_op jit(solution)/shard_map/all_gather | solution.py:35
  332.0 22.7 %all-to-all-done = bf16[256,4,2048]{2,0,1:T(8,128)(2,1)} async-done(((bf16[256,4,2048]{2,0,1:T(8,128)(2,1)}), bf16[256,4,2048]{2,0,1:T(8,128)(2,1)}, u32[]{:S(2)}, u32[]{:S(2)}) %all-to-all-start) | async-done | bytes 4194336 | tf_op jit(solution)/shard_map/all_to_all | solution.py:34
  354.6 17.6 %select_convert_fusion = (bf16[2048,2048]{1,0:T(8,128)(2,1)}, f32[2048,2048]{1,0:T(8,128)}) fusion(s32[2048]{0:T(1024)S(1)} %get-tuple-element.10, s32[2048]{0:T(1024)S(1)} %get-tuple-element.11, bf16[1024,2048]{1,0:T(8,128)(2,1)} %bitcast.1, bf16[1024,2048]{1,0:T(8,128)(2,1)} %all-gather.7.cloned.1.call-done), kind=kOutput, calls=%fused_computation | convolution fusion | flops 8602517504 | bytes 33570816 | tf_op jit(solution)/shard_map/dot_general | solution.py:36
  372.3 0.0 all-gather.9.cloned.1.call-update
  372.3 0.0 copy-start
  372.3 0.2 all-gather.11.cloned.1.call-start
  372.5 3.1 multiply_reduce_fusion
  375.7 197.5 %all-gather.9.cloned.1.call-done = bf16[8192,2048]{1,0:T(8,128)(2,1)} async-done(((bf16[2048,2048]{1,0:T(8,128)(2,1)}), bf16[8192,2048]{1,0:T(8,128)(2,1)}) %all-gather.9.cloned.1.call-update) | async-done | bytes 33554448 | tf_op jit(solution)/shard_map/all_gather | solution.py:49
  573.2 0.0 copy-done
  573.2 17.0 %fusion.1 = bf16[256,2048]{1,0:T(8,128)(2,1)} fusion(bf16[256,8192]{1,0:T(8,128)(2,1)} %all-gather.5.cloned.1.call-done, bf16[8192,2048]{1,0:T(8,128)(2,1)} %all-gather.9.cloned.1.call-done, bf16[256,2048]{1,0:T(8,128)(2,1)S(1)} %copy-done, f32[2048]{0:T(1024)S(1)} %select_multiply_fusion), kind=kOutput, calls=%fused_computation.11 | convolution fusion | flops 8592556032 | bytes 39854080 | tf_op jit(solution)/shard_map/dot_general | solution.py:47
  590.2 0.0 all-gather.11.cloned.1.call-update
  590.3 80.9 %all-gather.11.cloned.1.call-done = bf16[256,8192]{1,0:T(8,128)(2,1)} async-done(((bf16[256,2048]{1,0:T(8,128)(2,1)}), bf16[256,8192]{1,0:T(8,128)(2,1)}) %all-gather.11.cloned.1.call-update) | async-done | bytes 4194320 | tf_op jit(solution)/shard_map/all_gather | solution.py:56
  671.2 16.6 %convolution_convert_fusion = bf16[256,2048]{1,0:T(8,128)(2,1)} fusion(bf16[256,8192]{1,0:T(8,128)(2,1)} %all-gather.11.cloned.1.call-done, bf16[2048,8192]{1,0:T(8,128)(2,1)} %param.7), kind=kOutput, calls=%fused_computation.12 | convolution fusion | flops 8590458880 | bytes 38797312 | tf_op jit(solution)/shard_map/dot_general | solution.py:55
  (4 shorter events, 0.0 us)
Async XLA Ops:
  7.2 176.7 %reduce-scatter.2.cloned.1.call-start = ((), (), s32[]{:S(2)}) async-start(), calls=%async_computation.2 | async-start | bytes 10485760 | tf_op jit(solution)/shard_map/reduce_scatter | solution.py:23
  38.9 237.2 %all-gather.5.cloned.1.call-start = ((), (), s32[]{:S(2)}) async-start(), calls=%async_computation.3 | async-start | bytes 5242880 | tf_op jit(solution)/shard_map/all_gather | solution.py:8
  194.8 137.1 %all-gather.7.cloned.1.call-start = ((), (), s32[]{:S(2)}) async-start(), calls=%async_computation.4 | async-start | bytes 5242880 | tf_op jit(solution)/shard_map/all_gather | solution.py:35
  280.8 73.8 %all-to-all-start = ((bf16[256,4,2048]{2,0,1:T(8,128)(2,1)}), bf16[256,4,2048]{2,0,1:T(8,128)(2,1)}, u32[]{:S(2)}, u32[]{:S(2)}) async-start(bf16[256,4,2048]{2,0,1:T(8,128)(2,1)} %bitcast.14), calls=%async_computation.1 | async-start | bytes 8388608 | tf_op jit(solution)/shard_map/all_to_all | solution.py:34
  285.8 287.4 %all-gather.9.cloned.1.call-start = ((), (), s32[]{:S(2)}) async-start(), calls=%async_computation.5 | async-start | bytes 41943040 | tf_op jit(solution)/shard_map/all_gather | solution.py:49
  372.3 200.9 %copy-start = (bf16[256,2048]{1,0:T(8,128)(2,1)S(1)}, bf16[256,2048]{1,0:T(8,128)(2,1)}, u32[]{:S(2)}) copy-start(bf16[256,2048]{1,0:T(8,128)(2,1)} %fusion.2) | copy-start | bytes 3145732
  372.3 298.9 %all-gather.11.cloned.1.call-start = ((), (), s32[]{:S(2)}) async-start(), calls=%async_computation.6 | async-start | bytes 5242880 | tf_op jit(solution)/shard_map/all_gather | solution.py:56
Sparse Core Ops, SparseCore 0:
  39.0 144.7 reduce-scatter.1
  194.9 81.0 all-gather.4
  278.2 53.7 all-gather.6
  372.4 200.7 all-gather.8
  590.4 80.7 all-gather.10
where the time goes:
time: 695 us; the launch traced here: 694 us
  waiting for transfers between devices  573 us (82%)
  matrix products  68.7 us (10%)
  blocking collectives  19.2 us (3%)
  between operations  13.8 us (2%)
  other arithmetic  9.16 us (1%)
    all_gather x1, waiting for transfers between devices, shards(): lax.all_gather(off_diag, 'dp', axis=0, tiled=True)  198 us
    reduce_scatter x1, waiting for transfers between devices, shards(): lax.psum_scatter(partial_value, 'feat', scatter_dimension=1, tiled=True)  145 us
    all_gather x1, waiting for transfers between devices, shards(): lax.all_gather(grad_proj, 'feat', axis=1, tiled=True)  80.9 us
    all_gather x1, waiting for transfers between devices, whole_rows(): return lax.all_gather(centered, 'feat', axis=1, tiled=True)  80.5 us
    all_gather x1, waiting for transfers between devices, shards(): piece = lax.all_gather(centered, 'dp', axis=0, tiled=True)  46.1 us
    all_to_all x1, waiting for transfers between devices, shards(): lax.all_to_all(cent_full, 'dp', split_axis=1, concat_axis=0, tiled=True)  22.7 us
    dot_general x1, matrix products, shards(): lax.dot_general(cent_x, piece, (((0,), (0,)), ((), ())), preferred_elemen...  17.6 us
    dot_general x1, matrix products, shards(): jnp.dot(activated, weight, preferred_element_type=jnp.float32)  17.4 us
  transfers between devices with their start and end apart: 6, of which 6 were waited for; matrix products, arithmetic and copies ran while one was open for 1% of the time, Pallas kernels for 0%

commit v1 on v0

--- a/solution.py
+++ b/solution.py
@@ -2,6 +2,22 @@
 import jax.numpy as jnp
 from jax import lax
 from jax.sharding import PartitionSpec as P
+
+
+def gather_around(x, axis, dim):
+    ways, here, step = (lax.axis_size(axis), lax.axis_index(axis), x.shape[dim])
+    dims = [n * ways if d == dim else n for d, n in enumerate(x.shape)]
+    full = lax.dynamic_update_slice_in_dim(jnp.zeros(dims, x.dtype), x, here * step, axis=dim)
+    going_up = going_down = x
+    for far in range(1, ways // 2 + 1):
+        going_up = lax.ppermute(going_up, axis, [(d, (d + 1) % ways) for d in range(ways)])
+        full = lax.dynamic_update_slice_in_dim(full, going_up, (here - far) % ways * step, axis=dim)
+        if 2 * far < ways:
+            going_down = lax.ppermute(going_down, axis, [(d, (d - 1) % ways) for d in range(ways)])
+            full = lax.dynamic_update_slice_in_dim(
+                full, going_down, (here + far) % ways * step, axis=dim
+            )
+    return full
 
 
 def whole_rows(centered):
@@ -53,7 +69,7 @@
     active = jnp.where(spread < 1.0, 1.0 / spread, 0.0)
     grad_proj = (4.0 * scale_up * mixed - 25.0 * scale_up * active * cent_f).astype(jnp.bfloat16)
     grad_in = lax.dot_general(
-        lax.all_gather(grad_proj, "feat", axis=1, tiled=True),
+        gather_around(grad_proj, "feat", 1),
         weight,
         (((1,), (1,)), ((), ())),
         preferred_element_type=jnp.float32,

time: 695 us -> 691 us (level)
  waiting for transfers between devices: 573 us -> 559 us
  local copies, waits for them, and re-layouts: 4.79 us -> 11.9 us
    all_gather x1 -> x0, waiting for transfers between devices: 80.9 us -> none  [shards(): lax.all_gather(grad_proj, 'feat', axis=1, tiled=True)]
    ppermute x0 -> x3, waiting for transfers between devices: none -> 66.2 us  [the longest x2 46.1 us: gather_around(): lax.ppermute(going_up, axis, [(d, (d + 1) % ways) for d in range(ways)])]
  transfers between devices with their start and end apart: 6 -> 8, of which waited for: 6 -> 8; matrix products, arithmetic and copies ran while one was open for 1% -> 1% of each run, Pallas kernels for 0% -> 0%
where the time goes in v1:
time: 691 us; the launch traced here: 690 us
  waiting for transfers between devices  559 us (81%)
  matrix products  68.5 us (10%)
  blocking collectives  19.2 us (3%)
  between operations  13.8 us (2%)
  local copies, waits for them, and re-layouts  11.9 us (2%)
  other arithmetic  9.17 us (1%)
  starting transfers between devices  9.11 us (1%)
    all_gather x1, waiting for transfers between devices, shards(): lax.all_gather(off_diag, 'dp', axis=0, tiled=True)  198 us
    reduce_scatter x1, waiting for transfers between devices, shards(): lax.psum_scatter(partial_value, 'feat', scatter_dimension=1, tiled=True)  145 us
    all_gather x1, waiting for transfers between devices, whole_rows(): return lax.all_gather(centered, 'feat', axis=1, tiled=True)  80.5 us
    ppermute x2, waiting for transfers between devices, gather_around(): lax.ppermute(going_up, axis, [(d, (d + 1) % ways) for d in range(ways)])  46.1 us
    all_gather x1, waiting for transfers between devices, shards(): piece = lax.all_gather(centered, 'dp', axis=0, tiled=True)  46 us
    all_to_all x1, waiting for transfers between devices, shards(): lax.all_to_all(cent_full, 'dp', split_axis=1, concat_axis=0, tiled=True)  22.7 us
    ppermute x1, waiting for transfers between devices, gather_around(): lax.ppermute(going_down, axis, [(d, (d - 1) % ways) for d in range(ways)])  20.1 us
    dot_general x1, matrix products, shards(): lax.dot_general(cent_x, piece, (((0,), (0,)), ((), ())), preferred_elemen...  17.6 us
  transfers between devices with their start and end apart: 8, of which 8 were waited for; matrix products, arithmetic and copies ran while one was open for 1% of the time, Pallas kernels for 0%

profile of v1, /device:TPU:0, one launch (start us, length us, event | category | flops | bytes accessed | tf_op | source)
XLA Modules:
  0.0 690.3 jit_solution(15951524144099456728)
XLA Ops:
  7.2 0.0 reduce-scatter.2.cloned.1.call-start
  7.2 1.5 convert_reduce_fusion
  8.7 12.7 %all-reduce = (f32[2048]{0:T(1024)S(1)}, f32[2048]{0:T(1024)S(1)}) all-reduce(f32[2048]{0:T(1024)S(1)} %get-tuple-element.3, f32[2048]{0:T(1024)S(1)} %get-tuple-element.2), channel_id=1, replica_groups=mesh['groups'=2,'feat'=4,'dp'=4] {'dp'}, use_global_device_ids=true, to_apply=%region_3.0 | all-reduce | flops 4096 | bytes 32768 | tf_op jit(solution)/shard_map/psum | solution.py:33
  21.4 17.4 %fusion.9 = f32[256,8192]{1,0:T(8,128)} fusion(bf16[2048,8192]{1,0:T(8,128)(2,1)} %param.7, bf16[256,2048]{1,0:T(8,128)(2,1)} %param.4, f32[2048]{0:T(1024)} %param.6, f32[2048]{0:T(1024)} %param.5, f32[2048]{0:T(1024)S(1)} %get-tuple-element.7, f32[2048]{0:T(1024)S(1)} %get-tuple-element.6), kind=kOutput, calls=%fused_computation.20 | convolution fusion | flops 8593604608 | bytes 43024384 | tf_op jit(solution)/shard_map/dot_general | solution.py:38
  38.8 0.0 reduce-scatter.2.cloned.1.call-update
  38.9 0.0 all-gather.4.cloned.1.call-start
  38.9 144.9 %reduce-scatter.2.cloned.1.call-done = f32[256,2048]{1,0:T(8,128)} async-done(((f32[256,8192]{1,0:T(8,128)}), f32[256,2048]{1,0:T(8,128)}) %reduce-scatter.2.cloned.1.call-update) | async-done | bytes 2097168 | tf_op jit(solution)/shard_map/reduce_scatter | solution.py:39
  183.8 1.7 convert_reduce_fusion.1
  185.5 6.5 psum.23
  192.0 2.7 fusion.2
  194.8 0.0 all-gather.4.cloned.1.call-update
  194.8 0.0 all-gather.6.cloned.1.call-start
  194.9 0.7 all-gather.6.cloned.1.call-update
  195.6 80.5 %all-gather.4.cloned.1.call-done = bf16[256,8192]{1,0:T(8,128)(2,1)} async-done(((bf16[256,2048]{1,0:T(8,128)(2,1)}), bf16[256,8192]{1,0:T(8,128)(2,1)}) %all-gather.4.cloned.1.call-update) | async-done | bytes 4194320 | tf_op jit(solution)/shard_map/all_gather | solution.py:24
  276.0 4.8 copy.9
  280.8 4.9 all-to-all-start
  285.8 0.2 all-gather.8.cloned.1.call-start
  286.0 46.0 %all-gather.6.cloned.1.call-done = bf16[1024,2048]{1,0:T(8,128)(2,1)} async-done(((bf16[256,2048]{1,0:T(8,128)(2,1)}), bf16[1024,2048]{1,0:T(8,128)(2,1)}) %all-gather.6.cloned.1.call-update) | async-done | bytes 4194320 | tf_op jit(solution)/shard_map/all_gather | solution.py:51
  332.0 22.7 %all-to-all-done = bf16[256,4,2048]{2,0,1:T(8,128)(2,1)} async-done(((bf16[256,4,2048]{2,0,1:T(8,128)(2,1)}), bf16[256,4,2048]{2,0,1:T(8,128)(2,1)}, u32[]{:S(2)}, u32[]{:S(2)}) %all-to-all-start) | async-done | bytes 4194336 | tf_op jit(solution)/shard_map/all_to_all | solution.py:50
  354.6 17.6 %select_convert_fusion = (bf16[2048,2048]{1,0:T(8,128)(2,1)}, f32[2048,2048]{1,0:T(8,128)}) fusion(s32[2048]{0:T(1024)S(1)} %get-tuple-element.12, s32[2048]{0:T(1024)S(1)} %get-tuple-element.13, bf16[1024,2048]{1,0:T(8,128)(2,1)} %bitcast.1, bf16[1024,2048]{1,0:T(8,128)(2,1)} %all-gather.6.cloned.1.call-done), kind=kOutput, calls=%fused_computation | convolution fusion | flops 8602517504 | bytes 33570816 | tf_op jit(solution)/shard_map/dot_general | solution.py:52
  372.3 0.0 all-gather.8.cloned.1.call-update
  372.3 0.0 copy-start
  372.3 3.2 multiply_reduce_fusion
  375.5 197.7 %all-gather.8.cloned.1.call-done = bf16[8192,2048]{1,0:T(8,128)(2,1)} async-done(((bf16[2048,2048]{1,0:T(8,128)(2,1)}), bf16[8192,2048]{1,0:T(8,128)(2,1)}) %all-gather.8.cloned.1.call-update) | async-done | bytes 33554448 | tf_op jit(solution)/shard_map/all_gather | solution.py:65
  573.2 0.0 copy-start.1
  573.2 2.6 broadcast_in_dim.8
  575.8 0.0 copy-done
  575.8 1.1 copy-done.1
  576.9 16.8 %constant_dynamic-update-slice_fusion.3 = (bf16[256,8192]{1,0:T(8,128)(2,1)}, bf16[256,2048]{1,0:T(8,128)(2,1)}) fusion(bf16[256,8192]{1,0:T(8,128)(2,1)} %broadcast_in_dim.8, s32[]{:T(128)S(6)} %select_n.41, bf16[256,2048]{1,0:T(8,128)(2,1)S(1)} %copy-done, f32[2048]{0:T(1024)S(1)} %select_multiply_fusion, bf16[256,8192]{1,0:T(8,128)(2,1)S(1)} %copy-done.1, ...), kind=kOutput, calls=%fused_computation.36 | convolution fusion | flops 8592556032 | bytes 40902660 | tf_op jit(solution)/shard_map/dot_general | solution.py:63
  593.7 1.5 collective-permute-start
  595.2 2.3 collective-permute-start.1
  597.5 24.2 %collective-permute-done = bf16[256,2048]{1,0:T(8,128)(2,1)S(1)} collective-permute-done((bf16[256,2048]{1,0:T(8,128)(2,1)}, bf16[256,2048]{1,0:T(8,128)(2,1)S(1)}, u32[]{:S(2)}, u32[]{:S(2)}) %collective-permute-start) | collective-permute-done | bytes 1048608 | tf_op jit(solution)/shard_map/ppermute | solution.py:13
  621.7 0.0 collective-permute-start.2
  621.7 1.2 constant_dynamic-update-slice_fusion.2
  622.9 20.1 %collective-permute-done.1 = bf16[256,2048]{1,0:T(8,128)(2,1)S(1)} collective-permute-done((bf16[256,2048]{1,0:T(8,128)(2,1)}, bf16[256,2048]{1,0:T(8,128)(2,1)S(1)}, u32[]{:S(2)}, u32[]{:S(2)}) %collective-permute-start.1) | collective-permute-done | bytes 1048608 | tf_op jit(solution)/shard_map/ppermute | solution.py:16
  643.0 1.1 constant_dynamic-update-slice_fusion.1
  644.1 21.9 %collective-permute-done.2 = bf16[256,2048]{1,0:T(8,128)(2,1)S(1)} collective-permute-done((bf16[256,2048]{1,0:T(8,128)(2,1)S(1)}, bf16[256,2048]{1,0:T(8,128)(2,1)S(1)}, u32[]{:S(2)}, u32[]{:S(2)}) %collective-permute-start.2) | collective-permute-done | bytes 1048608 | tf_op jit(solution)/shard_map/ppermute | solution.py:13
  666.0 1.1 constant_dynamic-update-slice_fusion
  667.1 16.6 %convolution_convert_fusion = bf16[256,2048]{1,0:T(8,128)(2,1)} fusion(bf16[256,8192]{1,0:T(8,128)(2,1)} %constant_dynamic-update-slice_fusion, bf16[2048,8192]{1,0:T(8,128)(2,1)} %param.7), kind=kOutput, calls=%fused_computation.12 | convolution fusion | flops 8590458880 | bytes 38797312 | tf_op jit(solution)/shard_map/dot_general | solution.py:71
  (4 shorter events, 0.0 us)
Async XLA Ops:
  7.2 176.7 %reduce-scatter.2.cloned.1.call-start = ((), (), s32[]{:S(2)}) async-start(), calls=%async_computation.2 | async-start | bytes 10485760 | tf_op jit(solution)/shard_map/reduce_scatter | solution.py:39
  38.9 237.2 %all-gather.4.cloned.1.call-start = ((), (), s32[]{:S(2)}) async-start(), calls=%async_computation.3 | async-start | bytes 5242880 | tf_op jit(solution)/shard_map/all_gather | solution.py:24
  194.8 137.2 %all-gather.6.cloned.1.call-start = ((), (), s32[]{:S(2)}) async-start(), calls=%async_computation.4 | async-start | bytes 5242880 | tf_op jit(solution)/shard_map/all_gather | solution.py:51
  280.8 73.8 %all-to-all-start = ((bf16[256,4,2048]{2,0,1:T(8,128)(2,1)}), bf16[256,4,2048]{2,0,1:T(8,128)(2,1)}, u32[]{:S(2)}, u32[]{:S(2)}) async-start(bf16[256,4,2048]{2,0,1:T(8,128)(2,1)} %bitcast.14), calls=%async_computation.1 | async-start | bytes 8388608 | tf_op jit(solution)/shard_map/all_to_all | solution.py:50
  285.8 287.4 %all-gather.8.cloned.1.call-start = ((), (), s32[]{:S(2)}) async-start(), calls=%async_computation.5 | async-start | bytes 41943040 | tf_op jit(solution)/shard_map/all_gather | solution.py:65
  372.3 203.5 %copy-start = (bf16[256,2048]{1,0:T(8,128)(2,1)S(1)}, bf16[256,2048]{1,0:T(8,128)(2,1)}, u32[]{:S(2)}) copy-start(bf16[256,2048]{1,0:T(8,128)(2,1)} %fusion.2) | copy-start | bytes 3145732
  573.2 3.7 copy-start.1
  593.7 28.0 %collective-permute-start = (bf16[256,2048]{1,0:T(8,128)(2,1)}, bf16[256,2048]{1,0:T(8,128)(2,1)S(1)}, u32[]{:S(2)}, u32[]{:S(2)}) collective-permute-start(bf16[256,2048]{1,0:T(8,128)(2,1)} %get-tuple-element.11), channel_id=1, source_target_pairs={{0,4},{4,8},{8,12},{12,0},{1,5},{5,9},{9,13},{13,1},{2,6},{6,10},{... | collective-permute-start | bytes 3145736 | tf_op jit(solution)/shard_map/ppermute | solution.py:13
  595.2 47.8 %collective-permute-start.1 = (bf16[256,2048]{1,0:T(8,128)(2,1)}, bf16[256,2048]{1,0:T(8,128)(2,1)S(1)}, u32[]{:S(2)}, u32[]{:S(2)}) collective-permute-start(bf16[256,2048]{1,0:T(8,128)(2,1)} %get-tuple-element.11), channel_id=1, source_target_pairs={{0,12},{4,0},{8,4},{12,8},{1,13},{5,1},{9,5},{13,9},{2,14},{6,2},{... | collective-permute-start | bytes 3145736 | tf_op jit(solution)/shard_map/ppermute | solution.py:16
  621.7 44.3 %collective-permute-start.2 = (bf16[256,2048]{1,0:T(8,128)(2,1)S(1)}, bf16[256,2048]{1,0:T(8,128)(2,1)S(1)}, u32[]{:S(2)}, u32[]{:S(2)}) collective-permute-start(bf16[256,2048]{1,0:T(8,128)(2,1)S(1)} %collective-permute-done), channel_id=1, source_target_pairs={{0,4},{4,8},{8,12},{12,0},{1,5},{5,9},{9,13},{13,1},{2,6},{6,10},{... | collective-permute-start | bytes 3145736 | tf_op jit(solution)/shard_map/ppermute | solution.py:13
Sparse Core Ops, SparseCore 0:
  39.0 144.7 reduce-scatter.1
  194.9 81.0 all-gather.3
  278.2 53.7 all-gather.5
  372.4 200.7 all-gather.7
